TPU v7x, 512 devices: a whole 4x4x16 slice. The times are simulated.
512 devices in a mesh: ctx: 32 (over z_lo, y), head: 16 (over x, z_hi, core).
Axes of the slice: x: 4, y: 4, z: 16 (z_hi: 2, z_lo: 8; z = z_hi * 8 + z_lo), core: 2. Of those that a mesh axis runs over, the one named last changes fastest.
Arguments:
- q_nope: bfloat16 [4, 16384], P(None, 'head'), may hold values from -6 to 6
- q_rope: bfloat16 [4, 8192], P(None, 'head'), may hold values from -6 to 6
- latent_cache: bfloat16 [4, 16384, 512], P(None, 'ctx'), may hold values from -6 to 6
- rope_keys: bfloat16 [4, 64, 16384], P(None, None, 'ctx'), may hold values from -240 to 240
- lengths: int32 [4], replicated, may hold values from 2 to 16384, as said below
- w_uk: bfloat16 [128, 128, 512], P('head'), may hold values from -0.5 to 0.5
- w_uv: bfloat16 [128, 512, 128], P('head'), may hold values from -0.25 to 0.25
- w_o: bfloat16 [16384, 7168], P('head', 'ctx'), may hold values from -0.046875 to 0.046875
Outputs:
- layer_out: bfloat16 [4, 7168], P(None, 'ctx')
Inputs may be any that keep to these rules, and one draw needn't show every extreme that they name: `lengths`: every sequence has at least two valid positions, and some sequence fills the whole capacity 16384.
All inputs are finite; a program needn't handle non-finite values.
Results may differ from a plain program's by a relative error of at most 0.014.
Values may be sent and summed in bfloat16 or wider, within the bound.
A program may use at most 64 MiB of HBM per device.

v0:
```python
import jax
import jax.numpy as jnp
from jax import lax
from jax.sharding import PartitionSpec as P


def joined(shard, axis, combine):
    everything = jax.tree.map(lambda part: lax.all_gather(part, axis), shard)
    leading = jax.tree.map(lambda part: part[0], everything)

    def lap(k, so_far):
        return combine(so_far, jax.tree.map(lambda part: part[k], everything))

    return lax.fori_loop(1, lax.axis_size(axis), lap, leading)


def combine_partials(first, second):
    peak = jnp.maximum(first[0], second[0])
    scale_a = jnp.exp(first[0] - peak)
    scale_b = jnp.exp(second[0] - peak)
    total = first[1] * scale_a + second[1] * scale_b
    summed = first[2] * scale_a[..., None] + second[2] * scale_b[..., None]
    return (peak, total, summed)


def on_device(q_nope, q_rope, latent_cache, rope_keys, lengths, w_uk, w_uv, w_o):
    rows = q_nope.shape[0]
    heads = w_uk.shape[0]
    nope = w_uk.shape[1]
    rope = rope_keys.shape[1]
    span = latent_cache.shape[1]
    vwidth = w_uv.shape[2]
    scale = (nope + rope) ** (-0.5)
    q_abs = jnp.einsum(
        "rhn,hnc->rhc", q_nope.reshape(rows, heads, nope), w_uk, preferred_element_type=jnp.float32
    ).astype(jnp.bfloat16)
    rotary = q_rope.reshape(rows, heads, rope)
    offset = lax.axis_index("ctx") * span
    valid = (offset + jnp.arange(span, dtype=jnp.int32))[None, :] < lengths[:, None]
    scores = jnp.einsum("rhc,rtc->rht", q_abs, latent_cache, preferred_element_type=jnp.float32)
    scores = (
        scores + jnp.einsum("rhp,rpt->rht", rotary, rope_keys, preferred_element_type=jnp.float32)
    ) * scale
    scores = jnp.where(valid[:, None, :], scores, jnp.float32(-1e30))
    peak = jnp.max(scores, axis=2)
    weights = jnp.where(valid[:, None, :], jnp.exp(scores - peak[..., None]), jnp.float32(0.0))
    total = jnp.sum(weights, axis=2)
    summed = jnp.einsum(
        "rht,rtc->rhc",
        weights.astype(jnp.bfloat16),
        latent_cache,
        preferred_element_type=jnp.float32,
    )
    peak, total, summed = (peak, total, summed)
    peak, total, summed = joined((peak, total, summed), "ctx", combine_partials)
    attended = (summed / total[..., None]).astype(jnp.bfloat16)
    head_values = jnp.einsum("rhc,hcv->rhv", attended, w_uv, preferred_element_type=jnp.float32)
    head_values = head_values.astype(jnp.bfloat16).reshape(rows, heads * vwidth)
    partial_out = jnp.dot(head_values, w_o, preferred_element_type=jnp.float32)
    return lax.psum(partial_out, "head").astype(jnp.bfloat16)


def solution(mesh):
    placed = (
        P(None, "head"),
        P(None, "head"),
        P(None, "ctx", None),
        P(None, None, "ctx"),
        P(),
        P("head", None, None),
        P("head", None, None),
        P("head", "ctx"),
    )
    return jax.shard_map(
        on_device, mesh=mesh, in_specs=placed, out_specs=P(None, "ctx"), check_vma=False
    )
```

profile of v0, /device:TPU:1, one launch (start us, length us, event | category | flops | bytes accessed | tf_op | source)
XLA Modules:
  0.0 351.3 jit_solution(16708547603916031150)
XLA Ops:
  6.5 0.0 copy-start
  6.5 0.9 reshape.41
  7.5 0.7 broadcast_compare_fusion
  8.2 1.5 fusion.19
  9.7 0.6 fusion.12
  10.3 0.0 copy-done.2
  10.3 0.2 fusion.23
  10.6 1.1 fusion.9
  11.6 0.0 all-gather.7.cloned.1.call-update
  11.7 0.2 fusion.8
  11.8 112.5 %all-gather.4 = f32[32,4,8]{2,1,0:T(4,128)S(1)} all-gather(f32[1,4,8]{2,1,0:T(4,128)S(1)} %bitcast.47), channel_id=3, replica_groups=mesh['ctx'=32,'head'=16] {'ctx'}, dimensions={0}, use_global_device_ids=true | all-gather | bytes 4224 | tf_op jit(solution)/shard_map/all_gather | solution.py:8
  124.3 98.6 %all-gather.3 = f32[32,4,8]{2,1,0:T(4,128)S(1)} all-gather(f32[1,4,8]{2,1,0:T(4,128)S(1)} %bitcast.46), channel_id=2, replica_groups=mesh['ctx'=32,'head'=16] {'ctx'}, dimensions={0}, use_global_device_ids=true | all-gather | bytes 4224 | tf_op jit(solution)/shard_map/all_gather | solution.py:8
  222.9 0.8 slice.19
  223.8 30.1 %while.19 = (s32[]{:T(128)}, f32[4,8]{1,0:T(4,128)S(1)}, f32[4,8]{1,0:T(4,128)S(1)}, f32[4,8,512]{2,1,0:T(8,128)S(1)}, f32[32,4,8]{2,1,0:T(4,128)S(1)}, /*index=...) while((s32[]{:T(128)}, f32[4,8]{1,0:T(4,128)S(1)}, ...), condition=%wide.region_3.4_spmd, body=%wide.region_2.3_spmd.sunk | while | flops 49349 | bytes 198031 | solution.py:14
  223.8 0.9 fusion.34
  224.7 0.9 fusion.34
  225.7 0.9 fusion.34
  226.7 0.9 fusion.34
  227.7 0.9 fusion.34
  228.6 0.9 fusion.34
  229.6 0.9 fusion.34
  230.6 0.9 fusion.34
  231.6 0.9 fusion.34
  232.5 0.9 fusion.34
  233.5 0.9 fusion.34
  234.5 0.9 fusion.34
  235.4 0.9 fusion.34
  236.4 0.9 fusion.34
  237.4 0.9 fusion.34
  238.4 0.9 fusion.34
  239.3 0.9 fusion.34
  240.3 0.9 fusion.34
  241.3 0.9 fusion.34
  242.3 0.9 fusion.34
  243.2 0.9 fusion.34
  244.2 0.9 fusion.34
  245.2 0.9 fusion.34
  246.1 0.9 fusion.34
  247.1 0.9 fusion.34
  248.1 0.9 fusion.34
  249.1 0.9 fusion.34
  250.0 0.9 fusion.34
  251.0 0.9 fusion.34
  252.0 0.9 fusion.34
  253.0 0.9 fusion.34
  253.9 0.1 divide_convert_fusion
  254.0 1.4 fusion.6
  255.4 89.1 %psum.7 = bf16[4,224]{1,0:T(4,128)(2,1)} all-reduce(f32[4,224]{1,0:T(4,128)S(1)} %fusion.6), channel_id=1, replica_groups=mesh['ctx'=32,'head'=16] {'head'}, use_global_device_ids=true, to_apply=%region_4.5 | all-reduce | flops 896 | bytes 5376 | tf_op jit(solution)/shard_map/psum | solution.py:60
  (40 shorter events, 0.8 us)
Async XLA Ops:
  6.5 3.1 copy-start
  6.5 3.8 %copy-start.2 = (bf16[4,64,512]{2,1,0:T(8,128)(2,1)S(1)}, bf16[4,64,512]{2,1,0:T(8,128)(2,1)}, u32[]{:S(2)}) copy-start(bf16[4,64,512]{2,1,0:T(8,128)(2,1)} %param.13) | copy-start | bytes 786436
  6.5 216.4 %all-gather.7.cloned.1.call-start = ((), (), s32[]{:S(2)}) async-start(), calls=%async_computation | async-start | bytes 2162688 | tf_op jit(solution)/shard_map/all_gather | solution.py:8
  10.6 243.4 %copy-start.1 = (bf16[8,512,128]{2,1,0:T(8,128)(2,1)S(1)}, bf16[8,512,128]{2,1,0:T(8,128)(2,1)}, u32[]{:S(2)}) copy-start(bf16[8,512,128]{2,1,0:T(8,128)(2,1)} %param.16) | copy-start | bytes 3145732
Sparse Core Ops, SparseCore 0:
  11.8 209.2 all-gather.6
where the time goes:
time: 353 us; the launch traced here: 351 us
  blocking collectives  300 us (85%)
  other arithmetic  30.4 us (9%)
  between operations  13.4 us (4%)
  matrix products  4.8 us (1%)
    all_gather x2, blocking collectives, joined(): everything = jax.tree.map(lambda part: lax.all_gather(part, axis), shard)  211 us
    psum x1, blocking collectives, on_device(): return lax.psum(partial_out, 'head').astype(jnp.bfloat16)  89.1 us
    add x31, other arithmetic, combine_partials(): summed = first[2] * scale_a[..., None] + second[2] * scale_b[..., None]  28.6 us
  transfers between devices with their start and end apart: 1, of which 0 were waited for; matrix products, arithmetic and copies ran while one was open for 0% of the time, Pallas kernels for 0%

commit v1 on v0

v1 whole, which is shorter than its diff:
```python
import functools

import jax
import jax.numpy as jnp
from jax import lax
from jax.experimental import pallas as pl
from jax.experimental.pallas import tpu as pltpu
from jax.sharding import PartitionSpec as P

MESH = pl.DeviceIdType.MESH
F32, BF16 = jnp.float32, jnp.bfloat16
LOW = -1e30
NT = (((1,), (1,)), ((), ()))
NN = (((1,), (0,)), ((), ()))


def dot(a, b, dims=NN):
    return lax.dot_general(a, b, dims, preferred_element_type=F32)


def iota(shape, dim):
    return lax.broadcasted_iota(jnp.int32, shape, dim)


def kernel(
    ny, nz, nhead,
    qn_hbm, qr_hbm, lat_hbm, keys_hbm, len_hbm, wuk_hbm, wuv_hbm, wo_hbm,
    out_ref,
    qn, qr, lat, keys, lens, wuk, wuv, wo,
    ysum, ystat, zsum, zstat, terms,
    in_sem, ysend, yrecv, zsend, zrecv, hsend, hrecv,
):
    rows, span, latent = lat.shape
    heads, nope, _ = wuk.shape
    rope = keys.shape[1]
    vwidth = wuv.shape[2]
    pairs = rows * heads
    ctx, head = lax.axis_index("ctx"), lax.axis_index("head")

    loads = [
        pltpu.make_async_copy(src, dst, in_sem.at[n])
        for n, (src, dst) in enumerate(
            [(qn_hbm, qn), (wuk_hbm, wuk), (qr_hbm, qr), (len_hbm, lens)]
            + [(keys_hbm, keys)]
            + [(lat_hbm.at[r], lat.at[r]) for r in range(rows)]
            + [(wuv_hbm, wuv), (wo_hbm, wo)]
        )
    ]
    for load in loads:
        load.start()
    l_qn, l_wuk, l_qr, l_len, l_keys = loads[:5]
    l_lat, l_wuv, l_wo = loads[5 : 5 + rows], loads[5 + rows], loads[6 + rows]

    ypeers = [{"ctx": ctx // ny * ny + lax.rem(ctx + k, ny), "head": head} for k in range(1, ny)]
    zpeers = [{"ctx": lax.rem(ctx + k * ny, ny * nz), "head": head} for k in range(1, nz)]
    hpeers = [{"ctx": ctx, "head": lax.rem(head + k, nhead)} for k in range(1, nhead)]
    barrier = pltpu.get_barrier_semaphore()
    for peer in zpeers + hpeers + ypeers:
        pl.semaphore_signal(barrier, inc=1, device_id=peer, device_id_type=MESH)

    l_qn.wait()
    q = qn[...].astype(F32)
    own = iota((heads, heads * nope), 1) // nope == iota((heads, heads * nope), 0)
    q = jnp.concatenate([jnp.where(own, q[r : r + 1], 0.0) for r in range(rows)], axis=0)
    l_wuk.wait()
    q_abs = dot(q.astype(BF16), wuk[...].reshape(heads * nope, latent))
    l_qr.wait()
    q = qr[...].astype(F32)
    own = iota((heads, heads * rope), 1) // rope == iota((heads, heads * rope), 0)
    q = jnp.concatenate([jnp.where(own, q[r : r + 1], 0.0) for r in range(rows)], axis=0)
    rotary = sum(q[:, n * 2 * rope : (n + 1) * 2 * rope] for n in range(heads // 2))

    l_len.wait()
    l_keys.wait()
    position = iota((heads, span), 1) + ctx * span
    scale = (nope + rope) ** -0.5
    peaks, totals, sums = [], [], []
    for r in range(rows):
        l_lat[r].wait()
        mine = slice(r * heads, (r + 1) * heads)
        s = dot(q_abs[mine].astype(BF16), lat[r], NT)
        s += dot(rotary[mine].astype(BF16), jnp.concatenate([keys[r], keys[r]], axis=0))
        valid = position < lens[r]
        s = jnp.where(valid, s * scale, LOW)
        peak = jnp.max(s, axis=1, keepdims=True)
        w = jnp.where(valid, jnp.exp(s - peak), 0.0)
        peaks.append(peak)
        totals.append(jnp.sum(w, axis=1, keepdims=True))
        sums.append(dot(w.astype(BF16), lat[r]))
    peak, total, summed = (jnp.concatenate(x, axis=0) for x in (peaks, totals, sums))

    l_wuv.wait()
    which = lax.rem(iota((pairs, latent), 0), heads)
    values = sum(
        dot(jnp.where(which == h, summed, 0.0).astype(BF16), wuv[h]) for h in range(heads)
    )

    lanes = 128
    eye = lax.rem(iota((pairs, lanes), 1), pairs) == iota((pairs, lanes), 0)
    per = lanes // pairs

    def as_row(column):
        return jnp.sum(jnp.where(eye, column, 0.0), axis=0, keepdims=True)

    def put(sums_ref, stat_ref, values, peak, total):
        sums_ref[pl.ds(0, pairs), :] = values.astype(BF16)
        stat_ref[pl.ds(0, 1), pl.ds(0, lanes)] = peak
        stat_ref[pl.ds(0, 1), pl.ds(lanes, lanes)] = total

    def exchange(sums_ref, stat_ref, peers, send, recv):
        copies = []
        for k, peer in reversed(list(enumerate(peers))):
            for j, (src, dst) in enumerate(
                [
                    (stat_ref.at[pl.ds(0, 1)], stat_ref.at[pl.ds(k + 1, 1)]),
                    (sums_ref.at[pl.ds(0, pairs)], sums_ref.at[pl.ds((k + 1) * pairs, pairs)]),
                ]
            ):
                copies.append(
                    pltpu.make_async_remote_copy(
                        src_ref=src, dst_ref=dst, send_sem=send.at[2 * k + j],
                        recv_sem=recv.at[2 * k + j], device_id=peer, device_id_type=MESH,
                    )
                )
                copies[-1].start()
        return copies

    def combine(sums_ref, stat_ref, n, last):
        peaks = stat_ref[:, pl.ds(0, lanes)]
        totals = stat_ref[:, pl.ds(lanes, lanes)]
        peak = jnp.max(peaks, axis=0, keepdims=True)
        factor = jnp.exp(peaks - peak)
        total = jnp.sum(totals * factor, axis=0, keepdims=True)
        if last:
            factor = factor / total
        block = iota((n, lanes), 1) // pairs
        values = 0.0
        for g in range(n // per):
            pick = block + g * per == iota((n, lanes), 0)
            row = jnp.sum(jnp.where(pick, factor, 0.0), axis=0, keepdims=True)
            weights = jnp.where(eye, row, 0.0)
            high = weights.astype(BF16)
            low = (weights - high.astype(F32)).astype(BF16)
            part = sums_ref[pl.ds(g * lanes, lanes), :]
            values = values + dot(high, part) + dot(low, part)
        return values, peak, total

    pl.semaphore_wait(barrier, len(ypeers) + len(zpeers) + len(hpeers))
    put(ysum, ystat, values, as_row(peak), as_row(total))
    ycopies = exchange(ysum, ystat, ypeers, ysend, yrecv)
    for copy in ycopies:
        copy.wait_recv()
    values, peak, total = combine(ysum, ystat, ny, False)

    put(zsum, zstat, values, peak, total)
    zcopies = exchange(zsum, zstat, zpeers, zsend, zrecv)
    for copy in zcopies:
        copy.wait_recv()
    values, peak, total = combine(zsum, zstat, nz, True)

    l_wo.wait()
    wide = jnp.concatenate([values] * heads, axis=1)
    which = iota((pairs, heads * vwidth), 1) // vwidth == lax.rem(
        iota((pairs, heads * vwidth), 0), heads
    )
    wide = jnp.where(which, wide, 0.0).astype(BF16)
    term = dot(wide, wo[...], NT)
    term = jnp.concatenate(
        [jnp.sum(term[r * heads : (r + 1) * heads], axis=0, keepdims=True) for r in range(rows)],
        axis=0,
    )
    terms[pl.ds(0, rows), :] = term[:, :lanes]
    terms[pl.ds(rows, rows), :] = jnp.concatenate(
        [term[:, lanes:], jnp.zeros((rows, 2 * lanes - term.shape[1]), F32)], axis=1
    )
    hcopies = []
    for k, peer in reversed(list(enumerate(hpeers))):
        hcopies.append(
            pltpu.make_async_remote_copy(
                src_ref=terms.at[pl.ds(0, 2 * rows)],
                dst_ref=terms.at[pl.ds((k + 1) * 2 * rows, 2 * rows)],
                send_sem=hsend.at[k], recv_sem=hrecv.at[k], device_id=peer, device_id_type=MESH,
            )
        )
        hcopies[-1].start()
    for copy in hcopies:
        copy.wait_recv()
    whole = sum(terms[pl.ds(k * 2 * rows, 2 * rows), :] for k in range(nhead))
    whole = jnp.concatenate([whole[:rows], whole[rows:]], axis=1)
    out_ref[...] = whole[:, : out_ref.shape[1]].astype(out_ref.dtype)
    for copy in ycopies + zcopies + hcopies:
        copy.wait_send()


def on_device(ny, nz, nhead, q_nope, q_rope, latent_cache, rope_keys, lengths, w_uk, w_uv, w_o):
    rows, heads = q_nope.shape[0], w_uk.shape[0]
    pairs, vwidth, width = rows * heads, w_uv.shape[2], w_o.shape[1]
    w_o = w_o.T
    args = (q_nope, q_rope, latent_cache, rope_keys, lengths, w_uk, w_uv, w_o)
    scratch = [
        pltpu.SMEM(a.shape, a.dtype) if a is lengths else pltpu.VMEM(a.shape, a.dtype) for a in args
    ]
    scratch += [
        pltpu.VMEM((ny * pairs, vwidth), BF16),
        pltpu.VMEM((ny, 256), F32),
        pltpu.VMEM((nz * pairs, vwidth), BF16),
        pltpu.VMEM((nz, 256), F32),
        pltpu.VMEM((nhead * 2 * rows, 128), F32),
        pltpu.SemaphoreType.DMA((len(args) + rows - 1,)),
    ]
    for n in (2 * (ny - 1), 2 * (nz - 1), nhead - 1):
        scratch += [pltpu.SemaphoreType.DMA((n,))] * 2
    return pl.pallas_call(
        functools.partial(kernel, ny, nz, nhead),
        out_shape=jax.ShapeDtypeStruct((rows, width), BF16),
        in_specs=[pl.BlockSpec(memory_space=pl.ANY)] * len(args),
        out_specs=pl.BlockSpec(memory_space=pltpu.VMEM),
        scratch_shapes=scratch,
        compiler_params=pltpu.CompilerParams(
            collective_id=0, has_side_effects=True, vmem_limit_bytes=60 * 1024 * 1024
        ),
        name="decode",
    )(*args)


def solution(mesh):
    placed = (
        P(None, "head"),
        P(None, "head"),
        P(None, "ctx", None),
        P(None, None, "ctx"),
        P(),
        P("head", None, None),
        P("head", None, None),
        P("head", "ctx"),
    )
    nhead, nctx = mesh.shape["head"], mesh.shape["ctx"]
    ny = 4
    body = functools.partial(on_device, ny, nctx // ny, nhead)
    return jax.shard_map(
        body, mesh=mesh, in_specs=placed, out_specs=P(None, "ctx"), check_vma=False
    )
```

time: 353 us -> 40.3 us (0.11)
  blocking collectives: 300 us -> 0 us
  Pallas kernels: 0 us -> 38.8 us
  other arithmetic: 30.4 us -> 0 us
  between operations: 13.4 us -> 0.01 us
  matrix products: 4.8 us -> 0 us
    all_gather x2 -> x0, blocking collectives: 211 us -> none  [joined(): everything = jax.tree.map(lambda part: lax.all_gather(part, axis), shard)]
    psum x1 -> x0, blocking collectives: 89.1 us -> none  [on_device(): return lax.psum(partial_out, 'head').astype(jnp.bfloat16)]
    pallas_call x0 -> x1, Pallas kernels: none -> 38.8 us  [on_device(): pl.pallas_call(functools.partial(kernel, ny, nz, nhead), out_shape=jax.Sh...]
    add x63 -> x0, other arithmetic: 29.4 us -> none  [the longest x31 28.6 us: combine_partials(): summed = first[2] * scale_a[..., None] + second[2] * scale_b[..., None]]
    dot_general x5 -> x0, matrix products: 4.8 us -> none  [the longest x1 1.47 us: on_device(): jnp.einsum('rhn,hnc->rhc', q_nope.reshape(rows, heads, nope), w_uk, prefe...]
  transfers between devices with their start and end apart: 1 -> 0, of which waited for: 0 -> 0; matrix products, arithmetic and copies ran while one was open for 0% -> 0% of each run, Pallas kernels for 0% -> 0%
where the time goes in v1:
time: 40.3 us; the launch traced here: 40.1 us
  Pallas kernels  38.8 us (96%)
  local copies, waits for them, and re-layouts  1.26 us (3%)
    pallas_call x1, Pallas kernels, on_device(): pl.pallas_call(functools.partial(kernel, ny, nz, nhead), out_shape=jax.Sh...  38.8 us
    unnamed x1, local copies, waits for them, and re-layouts  1.26 us

profile of v1, /device:TPU:1, one launch (start us, length us, event | category | flops | bytes accessed | tf_op | source)
XLA Modules:
  0.0 40.1 jit_solution(7177664765376035053)
XLA Ops:
  0.0 38.8 %decode.1 = bf16[4,224]{1,0:T(4,128)(2,1)} custom-call(bf16[4,1024]{1,0:T(4,128)(2,1)} %qn_hbm.1, bf16[4,512]{1,0:T(4,128)(2,1)} %qr_hbm.1, bf16[4,512,512]{2,1,0:T(8,128)(2,1)} %lat_hbm.1, bf16[4,64,512]{2,1,0:T(8,128)(2,1)} %keys_hbm.1, s32[4]{0:T(128)} %len_hbm.1, bf16[8,128,512]{2,1,0:T(8,128)(2,1)} %wuk_hbm.1, bf16[8,512,128]{2,1,0:T(8,128)(2,1)} %wuv_hbm.1, ...), custom_call_target="tpu_custom_call" | custom-call | tf_op jit(solution)/shard_map/decode/pallas_call | solution.py:213
  38.8 1.3 %copy.10 = bf16[4,224]{1,0:T(4,128)(2,1)} copy(bf16[4,224]{1,0:T(4,128)(2,1)} %decode.1) | data formatting | bytes 3584

commit v2 on v1

v2 whole, which is shorter than its diff:
```python
import functools

import jax
import jax.numpy as jnp
from jax import lax
from jax.experimental import pallas as pl
from jax.experimental.pallas import tpu as pltpu
from jax.sharding import PartitionSpec as P

MESH = pl.DeviceIdType.MESH
F32, BF16 = jnp.float32, jnp.bfloat16
LOW = -1e30
NT = (((1,), (1,)), ((), ()))
NN = (((1,), (0,)), ((), ()))


def dot(a, b, dims=NN):
    return lax.dot_general(a, b, dims, preferred_element_type=F32)


def iota(shape, dim):
    return lax.broadcasted_iota(jnp.int32, shape, dim)


def kernel(
    ny, nz, nhead,
    qn_hbm, qr_hbm, lat_hbm, keys_hbm, len_hbm, wuk_hbm, wuv_hbm, wo_hbm,
    out_ref,
    qn, qr, lat, keys, lens, wuk, wuv, wo,
    by_head, mixed, ysum, ystat, zsum, zstat, terms,
    in_sem, ysend, yrecv, zsend, zrecv, hsend, hrecv,
):
    rows, span, latent = lat.shape
    heads, nope, _ = wuk.shape
    rope = keys.shape[1]
    vwidth = wuv.shape[2]
    pairs = rows * heads
    ctx, head = lax.axis_index("ctx"), lax.axis_index("head")

    loads = [
        pltpu.make_async_copy(src, dst, in_sem.at[n])
        for n, (src, dst) in enumerate(
            [(qn_hbm, qn)]
            + [(wuk_hbm.at[pl.ds(2 * h, 2)], wuk.at[pl.ds(2 * h, 2)]) for h in range(heads // 2)]
            + [(qr_hbm, qr), (len_hbm, lens), (keys_hbm, keys)]
            + [(lat_hbm.at[r], lat.at[r]) for r in range(rows)]
            + [(wuv_hbm, wuv), (wo_hbm, wo)]
        )
    ]
    for load in loads:
        load.start()
    l_qn, l_wuk = loads[0], loads[1 : 1 + heads // 2]
    l_qr, l_len, l_keys = loads[1 + heads // 2 : 4 + heads // 2]
    l_lat, l_wuv, l_wo = loads[-2 - rows : -2], loads[-2], loads[-1]

    ypeers = [{"ctx": ctx // ny * ny + lax.rem(ctx + k, ny), "head": head} for k in range(1, ny)]
    zpeers = [{"ctx": lax.rem(ctx + k * ny, ny * nz), "head": head} for k in range(1, nz)]
    hpeers = [{"ctx": ctx, "head": lax.rem(head + k, nhead)} for k in range(1, nhead)]
    barrier = pltpu.get_barrier_semaphore()
    for peer in zpeers + hpeers + ypeers:
        pl.semaphore_signal(barrier, inc=1, device_id=peer, device_id_type=MESH)

    l_qn.wait()
    q = qn[...].astype(F32)
    row_head = iota((heads, 1), 0)
    q_abs = 0.0
    for j in range(heads // 2):
        part = jnp.concatenate(
            [
                jnp.concatenate(
                    [
                        jnp.where(row_head == h, q[r : r + 1, h * nope : (h + 1) * nope], 0.0)
                        for h in (2 * j, 2 * j + 1)
                    ],
                    axis=1,
                )
                for r in range(rows)
            ],
            axis=0,
        ).astype(BF16)
        l_wuk[j].wait()
        q_abs += dot(part, wuk[pl.ds(2 * j, 2)].reshape(2 * nope, latent))
    l_qr.wait()
    q = qr[...].astype(F32)
    lane = iota((heads, 2 * rope), 1)
    own = (lane >= rope) == ((iota((heads, 2 * rope), 0) & 1) == 1)
    rotary = jnp.concatenate(
        [
            sum(
                jnp.where(
                    own & (row_head >> 1 == n), q[r : r + 1, n * 2 * rope : (n + 1) * 2 * rope], 0.0
                )
                for n in range(heads // 2)
            )
            for r in range(rows)
        ],
        axis=0,
    )

    l_len.wait()
    l_keys.wait()
    position = iota((heads, span), 1) + ctx * span
    scale = (nope + rope) ** -0.5
    valid = jnp.concatenate([position < lens[r] for r in range(rows)], axis=0)
    scores = []
    for r in range(rows):
        mine = slice(r * heads, (r + 1) * heads)
        both = jnp.concatenate([keys[r], keys[r]], axis=0)
        scores.append(dot(rotary[mine].astype(BF16), both))
    for r in range(rows):
        mine = slice(r * heads, (r + 1) * heads)
        l_lat[r].wait()
        scores[r] += dot(q_abs[mine].astype(BF16), lat[r], NT)
    scores = jnp.where(valid, jnp.concatenate(scores, axis=0) * scale, LOW)
    peak = jnp.max(scores, axis=1, keepdims=True)
    weights = jnp.where(valid, jnp.exp(scores - peak), 0.0)
    total = jnp.sum(weights, axis=1, keepdims=True)
    for r in range(rows):
        mine = slice(r * heads, (r + 1) * heads)
        part = dot(weights[mine].astype(BF16), lat[r])
        for n in range(latent // 128):
            by_head[n, pl.ds(r * heads, heads), :] = part[:, n * 128 : (n + 1) * 128]
    l_wuv.wait()
    values = []
    for h in range(heads):
        mine = [by_head[n, pl.ds(h, rows, stride=heads), :] for n in range(latent // 128)]
        values.append(dot(jnp.concatenate(mine, axis=1).astype(BF16), wuv[h]))
    for h in range(heads):
        mixed[pl.ds(h, rows, stride=heads), :] = values[h]
    values = mixed[...]
    lanes = 128
    eye = (iota((pairs, lanes), 1) & (pairs - 1)) == iota((pairs, lanes), 0)
    per = lanes // pairs

    def as_row(column):
        return jnp.sum(jnp.where(eye, column, 0.0), axis=0, keepdims=True)

    def put(sums_ref, stat_ref, values, peak, total):
        sums_ref[pl.ds(0, pairs), :] = values.astype(BF16)
        stat_ref[pl.ds(0, 1), pl.ds(0, lanes)] = peak
        stat_ref[pl.ds(0, 1), pl.ds(lanes, lanes)] = total

    def exchange(sums_ref, stat_ref, peers, send, recv):
        copies = []
        for k, peer in reversed(list(enumerate(peers))):
            for j, (src, dst) in enumerate(
                [
                    (stat_ref.at[pl.ds(0, 1)], stat_ref.at[pl.ds(k + 1, 1)]),
                    (sums_ref.at[pl.ds(0, pairs)], sums_ref.at[pl.ds((k + 1) * pairs, pairs)]),
                ]
            ):
                pltpu.make_async_remote_copy(
                    src_ref=src, dst_ref=dst, send_sem=send.at[j], recv_sem=recv.at[j],
                    device_id=peer, device_id_type=MESH,
                ).start()
        n = len(peers)
        return [
            pltpu.make_async_remote_copy(
                src_ref=ref, dst_ref=ref, send_sem=send.at[j], recv_sem=recv.at[j],
                device_id=peers[0], device_id_type=MESH,
            )
            for j, ref in enumerate([stat_ref.at[pl.ds(1, n)], sums_ref.at[pl.ds(pairs, n * pairs)]])
        ]

    def combine(sums_ref, stat_ref, n, last):
        peaks = stat_ref[:, pl.ds(0, lanes)]
        totals = stat_ref[:, pl.ds(lanes, lanes)]
        peak = jnp.max(peaks, axis=0, keepdims=True)
        factor = jnp.exp(peaks - peak)
        total = jnp.sum(totals * factor, axis=0, keepdims=True)
        if last:
            factor = factor / total
        block = iota((n, lanes), 1) >> (pairs.bit_length() - 1)
        values = 0.0
        for g in range(n // per):
            pick = block + g * per == iota((n, lanes), 0)
            row = jnp.sum(jnp.where(pick, factor, 0.0), axis=0, keepdims=True)
            weights = jnp.where(eye, row, 0.0)
            high = weights.astype(BF16)
            low = (weights - high.astype(F32)).astype(BF16)
            part = sums_ref[pl.ds(g * lanes, lanes), :]
            values = values + dot(high, part) + dot(low, part)
        return values, peak, total

    pl.semaphore_wait(barrier, len(ypeers) + len(zpeers) + len(hpeers))
    put(ysum, ystat, values, as_row(peak), as_row(total))
    ycopies = exchange(ysum, ystat, ypeers, ysend, yrecv)
    for copy in ycopies:
        copy.wait_recv()
    values, peak, total = combine(ysum, ystat, ny, False)

    put(zsum, zstat, values, peak, total)
    zcopies = exchange(zsum, zstat, zpeers, zsend, zrecv)
    for copy in zcopies:
        copy.wait_recv()
    values, peak, total = combine(zsum, zstat, nz, True)

    l_wo.wait()
    mixed[...] = values
    wide = [mixed[pl.ds(h, rows, stride=heads), :] for h in range(heads)]
    term = dot(jnp.concatenate(wide, axis=1).astype(BF16), wo[...], NT)
    terms[pl.ds(0, rows), :] = term[:, :lanes]
    terms[pl.ds(rows, rows), :] = jnp.concatenate(
        [term[:, lanes:], jnp.zeros((rows, 2 * lanes - term.shape[1]), F32)], axis=1
    )
    for k, peer in reversed(list(enumerate(hpeers))):
        pltpu.make_async_remote_copy(
            src_ref=terms.at[pl.ds(0, 2 * rows)],
            dst_ref=terms.at[pl.ds((k + 1) * 2 * rows, 2 * rows)],
            send_sem=hsend.at[0], recv_sem=hrecv.at[0], device_id=peer, device_id_type=MESH,
        ).start()
    others = terms.at[pl.ds(2 * rows, (nhead - 1) * 2 * rows)]
    hcopy = pltpu.make_async_remote_copy(
        src_ref=others, dst_ref=others, send_sem=hsend.at[0], recv_sem=hrecv.at[0],
        device_id=hpeers[0], device_id_type=MESH,
    )
    hcopy.wait_recv()
    whole = sum(terms[pl.ds(k * 2 * rows, 2 * rows), :] for k in range(nhead))
    whole = jnp.concatenate([whole[:rows], whole[rows:]], axis=1)
    out_ref[...] = whole[:, : out_ref.shape[1]].astype(out_ref.dtype)
    for copy in ycopies + zcopies + [hcopy]:
        copy.wait_send()


def on_device(ny, nz, nhead, q_nope, q_rope, latent_cache, rope_keys, lengths, w_uk, w_uv, w_o):
    rows, heads = q_nope.shape[0], w_uk.shape[0]
    pairs, vwidth, width = rows * heads, w_uv.shape[2], w_o.shape[1]
    w_o = w_o.T
    args = (q_nope, q_rope, latent_cache, rope_keys, lengths, w_uk, w_uv, w_o)
    scratch = [
        pltpu.SMEM(a.shape, a.dtype) if a is lengths else pltpu.VMEM(a.shape, a.dtype) for a in args
    ]
    scratch += [
        pltpu.VMEM((w_uv.shape[1] // 128, pairs, 128), F32),
        pltpu.VMEM((pairs, vwidth), F32),
        pltpu.VMEM((ny * pairs, vwidth), BF16),
        pltpu.VMEM((ny, 256), F32),
        pltpu.VMEM((nz * pairs, vwidth), BF16),
        pltpu.VMEM((nz, 256), F32),
        pltpu.VMEM((nhead * 2 * rows, 128), F32),
        pltpu.SemaphoreType.DMA((len(args) + rows + heads // 2 - 2,)),
    ]
    for n in (2, 2, 1):
        scratch += [pltpu.SemaphoreType.DMA((n,))] * 2
    return pl.pallas_call(
        functools.partial(kernel, ny, nz, nhead),
        out_shape=jax.ShapeDtypeStruct((rows, width), BF16),
        in_specs=[pl.BlockSpec(memory_space=pl.ANY)] * len(args),
        out_specs=pl.BlockSpec(memory_space=pltpu.VMEM),
        scratch_shapes=scratch,
        compiler_params=pltpu.CompilerParams(
            collective_id=0, has_side_effects=True, vmem_limit_bytes=32 * 1024 * 1024
        ),
        name="decode",
    )(*(pltpu.with_memory_space_constraint(a, pltpu.HBM) for a in args))


def solution(mesh):
    placed = (
        P(None, "head"),
        P(None, "head"),
        P(None, "ctx", None),
        P(None, None, "ctx"),
        P(),
        P("head", None, None),
        P("head", None, None),
        P("head", "ctx"),
    )
    nhead, nctx = mesh.shape["head"], mesh.shape["ctx"]
    ny = 4
    body = functools.partial(on_device, ny, nctx // ny, nhead)
    return jax.shard_map(
        body, mesh=mesh, in_specs=placed, out_specs=P(None, "ctx"), check_vma=False
    )
```

time: 40.3 us -> 38.3 us (0.950)
  Pallas kernels: 38.8 us -> 37.6 us
  local copies, waits for them, and re-layouts: 1.26 us -> 0.58 us
    pallas_call x1, Pallas kernels: 38.8 us -> 37.6 us  [on_device(): pl.pallas_call(functools.partial(kernel, ny, nz, nhead), out_shape=jax.Sh...]
    unnamed x1, local copies, waits for them, and re-layouts: 1.26 us -> 0.58 us
where the time goes in v2:
time: 38.3 us; the launch traced here: 38.2 us
  Pallas kernels  37.6 us (98%)
  local copies, waits for them, and re-layouts  0.58 us (2%)
    pallas_call x1, Pallas kernels, on_device(): pl.pallas_call(functools.partial(kernel, ny, nz, nhead), out_shape=jax.Sh...  37.6 us

profile of v2, /device:TPU:1, one launch (start us, length us, event | category | flops | bytes accessed | tf_op | source)
XLA Modules:
  0.0 38.2 jit_solution(796031087632100573)
XLA Ops:
  0.0 37.6 %decode.1 = bf16[4,224]{1,0:T(4,128)(2,1)S(1)} custom-call(bf16[4,1024]{1,0:T(4,128)(2,1)} %qn_hbm.1, bf16[4,512]{1,0:T(4,128)(2,1)} %qr_hbm.1, bf16[4,512,512]{2,1,0:T(8,128)(2,1)} %lat_hbm.1, bf16[4,64,512]{2,1,0:T(8,128)(2,1)} %keys_hbm.1, s32[4]{0:T(128)} %len_hbm.1, bf16[8,128,512]{2,1,0:T(8,128)(2,1)} %wuk_hbm.1, bf16[8,512,128]{2,1,0:T(8,128)(2,1)} %wuv_hbm.1, ...), custom_call_target="tpu_custom_call" | custom-call | tf_op jit(solution)/shard_map/decode/pallas_call | solution.py:245
  37.6 0.6 %copy.10 = bf16[4,224]{1,0:T(4,128)(2,1)} copy(bf16[4,224]{1,0:T(4,128)(2,1)S(1)} %decode.1) | data formatting | bytes 3584

commit v3 on v2

--- a/solution.py
+++ b/solution.py
@@ -28,7 +28,7 @@
     out_ref,
     qn, qr, lat, keys, lens, wuk, wuv, wo,
     by_head, mixed, ysum, ystat, zsum, zstat, terms,
-    in_sem, ysend, yrecv, zsend, zrecv, hsend, hrecv,
+    run_sem, border_sem, in_sem, ysend, yrecv, zsend, zrecv, hsend, hrecv,
 ):
     rows, span, latent = lat.shape
     heads, nope, _ = wuk.shape
@@ -36,6 +36,38 @@
     vwidth = wuv.shape[2]
     pairs = rows * heads
     ctx, head = lax.axis_index("ctx"), lax.axis_index("head")
+
+    y, z = lax.rem(ctx, ny), lax.div(ctx, ny)
+    half, core = lax.rem(lax.div(head, 2), 2), lax.rem(head, 2)
+    column = lax.div(head, 4)
+
+    def along(z):
+        return {"ctx": z * ny + y, "head": head}
+
+    def across(ctx, half, k, j):
+        x = lax.rem(column + k, nhead // 4)
+        return {"ctx": ctx, "head": x * 4 + half * 2 + lax.rem(core + j, 2)}
+
+    ypeers = [{"ctx": z * ny + lax.rem(y + k, ny), "head": head} for k in range(1, ny)]
+    zpeers = [along(lax.rem(z + k, nz)) for k in range(1, nz)]
+    order = [(k, j) for k in (2, 1, 3, 0) for j in (1, 0)]
+    hpeers = [across(ctx, 1 - half, k, j) for k, j in order]
+    hpeers += [across(ctx, half, k, j) for k, j in order if k + j]
+    beside = hpeers[len(order) :]
+    middle = (nz // 2 - 1, nz // 2)
+    at_middle = (z == middle[0]) | (z == middle[1])
+    at_border = z == (nz - 1) * (1 - half)
+    opposite = [across((nz - 1) * half * ny + y, 1 - half, k, j) for k, j in order]
+
+    def tell(semaphore, peers):
+        for peer in peers:
+            pl.semaphore_signal(semaphore, inc=1, device_id=peer, device_id_type=MESH)
+
+    barrier = pltpu.get_barrier_semaphore()
+    for place in middle:
+        pl.when(z != place)(functools.partial(tell, barrier, [along(place)]))
+    pl.when(at_border)(functools.partial(tell, barrier, opposite))
+    tell(barrier, ypeers + beside)
 
     loads = [
         pltpu.make_async_copy(src, dst, in_sem.at[n])
@@ -52,13 +84,6 @@
     l_qn, l_wuk = loads[0], loads[1 : 1 + heads // 2]
     l_qr, l_len, l_keys = loads[1 + heads // 2 : 4 + heads // 2]
     l_lat, l_wuv, l_wo = loads[-2 - rows : -2], loads[-2], loads[-1]
-
-    ypeers = [{"ctx": ctx // ny * ny + lax.rem(ctx + k, ny), "head": head} for k in range(1, ny)]
-    zpeers = [{"ctx": lax.rem(ctx + k * ny, ny * nz), "head": head} for k in range(1, nz)]
-    hpeers = [{"ctx": ctx, "head": lax.rem(head + k, nhead)} for k in range(1, nhead)]
-    barrier = pltpu.get_barrier_semaphore()
-    for peer in zpeers + hpeers + ypeers:
-        pl.semaphore_signal(barrier, inc=1, device_id=peer, device_id_type=MESH)
 
     l_qn.wait()
     q = qn[...].astype(F32)
@@ -142,7 +167,7 @@
 
     def exchange(sums_ref, stat_ref, peers, send, recv):
         copies = []
-        for k, peer in reversed(list(enumerate(peers))):
+        for k, peer in enumerate(peers):
             for j, (src, dst) in enumerate(
                 [
                     (stat_ref.at[pl.ds(0, 1)], stat_ref.at[pl.ds(k + 1, 1)]),
@@ -182,7 +207,15 @@
             values = values + dot(high, part) + dot(low, part)
         return values, peak, total
 
-    pl.semaphore_wait(barrier, len(ypeers) + len(zpeers) + len(hpeers))
+    heard = len(ypeers) + len(beside)
+    heard += at_middle.astype(jnp.int32) * len(zpeers) + at_border.astype(jnp.int32) * len(opposite)
+    pl.semaphore_wait(barrier, heard)
+
+    @pl.when(at_middle)
+    def _():
+        first = lax.div(z, nz // 2) * (nz // 2 + 1)
+        tell(run_sem, [along(first + k) for k in range(nz // 2 - 1)])
+
     put(ysum, ystat, values, as_row(peak), as_row(total))
     ycopies = exchange(ysum, ystat, ypeers, ysend, yrecv)
     for copy in ycopies:
@@ -190,6 +223,16 @@
     values, peak, total = combine(ysum, ystat, ny, False)
 
     put(zsum, zstat, values, peak, total)
+
+    @pl.when(jnp.logical_not(at_middle))
+    def _():
+        pl.semaphore_wait(run_sem, 1)
+
+    @pl.when(at_border)
+    def _():
+        tell(border_sem, opposite)
+        pl.semaphore_wait(border_sem, len(opposite))
+
     zcopies = exchange(zsum, zstat, zpeers, zsend, zrecv)
     for copy in zcopies:
         copy.wait_recv()
@@ -203,7 +246,7 @@
     terms[pl.ds(rows, rows), :] = jnp.concatenate(
         [term[:, lanes:], jnp.zeros((rows, 2 * lanes - term.shape[1]), F32)], axis=1
     )
-    for k, peer in reversed(list(enumerate(hpeers))):
+    for k, peer in enumerate(hpeers):
         pltpu.make_async_remote_copy(
             src_ref=terms.at[pl.ds(0, 2 * rows)],
             dst_ref=terms.at[pl.ds((k + 1) * 2 * rows, 2 * rows)],
@@ -238,6 +281,8 @@
         pltpu.VMEM((nz * pairs, vwidth), BF16),
         pltpu.VMEM((nz, 256), F32),
         pltpu.VMEM((nhead * 2 * rows, 128), F32),
+        pltpu.SemaphoreType.REGULAR,
+        pltpu.SemaphoreType.REGULAR,
         pltpu.SemaphoreType.DMA((len(args) + rows + heads // 2 - 2,)),
     ]
     for n in (2, 2, 1):

time: 38.3 us -> 35 us (0.914)
  Pallas kernels: 37.6 us -> 34.2 us
    pallas_call x1, Pallas kernels: 37.6 us -> 34.2 us  [on_device(): pl.pallas_call(functools.partial(kernel, ny, nz, nhead), out_shape=jax.Sh...]
where the time goes in v3:
time: 35 us; the launch traced here: 34.8 us
  Pallas kernels  34.2 us (98%)
  local copies, waits for them, and re-layouts  0.58 us (2%)
    pallas_call x1, Pallas kernels, on_device(): pl.pallas_call(functools.partial(kernel, ny, nz, nhead), out_shape=jax.Sh...  34.2 us

profile of v3, /device:TPU:1, one launch (start us, length us, event | category | flops | bytes accessed | tf_op | source)
XLA Modules:
  0.0 34.8 jit_solution(10905541030044823569)
XLA Ops:
  0.0 34.2 %decode.1 = bf16[4,224]{1,0:T(4,128)(2,1)S(1)} custom-call(bf16[4,1024]{1,0:T(4,128)(2,1)} %qn_hbm.1, bf16[4,512]{1,0:T(4,128)(2,1)} %qr_hbm.1, bf16[4,512,512]{2,1,0:T(8,128)(2,1)} %lat_hbm.1, bf16[4,64,512]{2,1,0:T(8,128)(2,1)} %keys_hbm.1, s32[4]{0:T(128)} %len_hbm.1, bf16[8,128,512]{2,1,0:T(8,128)(2,1)} %wuk_hbm.1, bf16[8,512,128]{2,1,0:T(8,128)(2,1)} %wuv_hbm.1, ...), custom_call_target="tpu_custom_call" | custom-call | tf_op jit(solution)/shard_map/decode/pallas_call | solution.py:290
  34.2 0.6 %copy.10 = bf16[4,224]{1,0:T(4,128)(2,1)} copy(bf16[4,224]{1,0:T(4,128)(2,1)S(1)} %decode.1) | data formatting | bytes 3584

commit v4 on v2

--- a/solution.py
+++ b/solution.py
@@ -27,8 +27,8 @@
     qn_hbm, qr_hbm, lat_hbm, keys_hbm, len_hbm, wuk_hbm, wuv_hbm, wo_hbm,
     out_ref,
     qn, qr, lat, keys, lens, wuk, wuv, wo,
-    by_head, mixed, ysum, ystat, zsum, zstat, terms,
-    in_sem, ysend, yrecv, zsend, zrecv, hsend, hrecv,
+    by_head, mixed, turned, asum, astat, bsum, bstat, terms,
+    parity_sem, other_sem, border_sem, run_sem, in_sem, asend, arecv, bsend, brecv, hsend, hrecv,
 ):
     rows, span, latent = lat.shape
     heads, nope, _ = wuk.shape
@@ -53,12 +53,42 @@
     l_qr, l_len, l_keys = loads[1 + heads // 2 : 4 + heads // 2]
     l_lat, l_wuv, l_wo = loads[-2 - rows : -2], loads[-2], loads[-1]
 
-    ypeers = [{"ctx": ctx // ny * ny + lax.rem(ctx + k, ny), "head": head} for k in range(1, ny)]
-    zpeers = [{"ctx": lax.rem(ctx + k * ny, ny * nz), "head": head} for k in range(1, nz)]
-    hpeers = [{"ctx": ctx, "head": lax.rem(head + k, nhead)} for k in range(1, nhead)]
+    y, z = lax.rem(ctx, ny), lax.div(ctx, ny)
+    half, core = lax.rem(lax.div(head, 2), 2), lax.rem(head, 2)
+    column, parity = lax.div(head, 4), lax.rem(z, 2)
+    partner = z + 1 - 2 * parity
+
+    def grid(z, k=0):
+        return {"ctx": z * ny + lax.rem(y + k, ny), "head": head}
+
+    def heads_at(z, half, k, j):
+        x = lax.rem(column + k, nhead // 4)
+        return {"ctx": z * ny + y, "head": x * 4 + half * 2 + lax.rem(core + j, 2)}
+
+    apeers = [grid(z_, k) for z_, k in [(partner, 2), (partner, 1), (partner, 3), (z, 2), (z, 1), (z, 3), (partner, 0)]]
+    bpeers = [grid(lax.rem(z + k, nz)) for k in range(2, nz, 2)]
+    order = [(k, j) for k in (2, 1, 3, 0) for j in (1, 0)]
+    distant = [heads_at(z, 1 - half, k, j) for k, j in order]
+    beside = [heads_at(z, half, k, j) for k, j in order if k + j]
+
+    upper = (z >= nz // 2).astype(jnp.int32)
+    middle = (z >= nz // 4) & (z < nz - nz // 4)
+    centre = (z == nz // 2 - 1) | (z == nz // 2)
+    end = (z == 0) | (z == nz - 1)
+    border = z == (nz - 1) * (1 - half)
+    opposite = [heads_at((nz - 1) * half, 1 - half, k, j) for k, j in order]
+    run = [grid(lax.rem(z + k, nz)) for k in range(1, nz)]
+
+    def tell(semaphore, peers):
+        for peer in peers:
+            pl.semaphore_signal(semaphore, inc=1, device_id=peer, device_id_type=MESH)
+
     barrier = pltpu.get_barrier_semaphore()
-    for peer in zpeers + hpeers + ypeers:
-        pl.semaphore_signal(barrier, inc=1, device_id=peer, device_id_type=MESH)
+    for place in (nz // 4, nz // 2):
+        pl.when(z != place + parity)(functools.partial(tell, barrier, [grid(place + parity)]))
+    pl.when(end)(functools.partial(tell, barrier, [grid(nz // 2 - 1 + upper)]))
+    pl.when(border)(functools.partial(tell, barrier, opposite))
+    tell(barrier, apeers + beside)
 
     l_qn.wait()
     q = qn[...].astype(F32)
@@ -109,7 +139,9 @@
         scores.append(dot(rotary[mine].astype(BF16), both))
     for r in range(rows):
         mine = slice(r * heads, (r + 1) * heads)
-        l_lat[r].wait()
+        if r % 2 == 0:
+            l_lat[r].wait()
+            l_lat[r + 1].wait()
         scores[r] += dot(q_abs[mine].astype(BF16), lat[r], NT)
     scores = jnp.where(valid, jnp.concatenate(scores, axis=0) * scale, LOW)
     peak = jnp.max(scores, axis=1, keepdims=True)
@@ -142,7 +174,7 @@
 
     def exchange(sums_ref, stat_ref, peers, send, recv):
         copies = []
-        for k, peer in reversed(list(enumerate(peers))):
+        for k, peer in enumerate(peers):
             for j, (src, dst) in enumerate(
                 [
                     (stat_ref.at[pl.ds(0, 1)], stat_ref.at[pl.ds(k + 1, 1)]),
@@ -182,43 +214,63 @@
             values = values + dot(high, part) + dot(low, part)
         return values, peak, total
 
-    pl.semaphore_wait(barrier, len(ypeers) + len(zpeers) + len(hpeers))
-    put(ysum, ystat, values, as_row(peak), as_row(total))
-    ycopies = exchange(ysum, ystat, ypeers, ysend, yrecv)
-    for copy in ycopies:
+    heard = len(apeers) + len(beside) + middle.astype(jnp.int32) * len(bpeers)
+    heard += centre.astype(jnp.int32) + border.astype(jnp.int32) * len(opposite)
+    pl.semaphore_wait(barrier, heard)
+    pl.when(middle)(functools.partial(tell, parity_sem, [grid(z - 2 + 4 * upper)]))
+    pl.when(centre)(functools.partial(tell, other_sem, [grid((nz - 1) * upper)]))
+
+    put(asum, astat, values, as_row(peak), as_row(total))
+    acopies = exchange(asum, astat, apeers, asend, arecv)
+    l_wo.wait()
+    turned[...] = wo[...].T
+    for copy in acopies:
         copy.wait_recv()
-    values, peak, total = combine(ysum, ystat, ny, False)
-
-    put(zsum, zstat, values, peak, total)
-    zcopies = exchange(zsum, zstat, zpeers, zsend, zrecv)
-    for copy in zcopies:
+    values, peak, total = combine(asum, astat, 2 * ny, False)
+    put(bsum, bstat, values, peak, total)
+    pl.when(jnp.logical_not(middle))(lambda: pl.semaphore_wait(parity_sem, 1))
+    bcopies = exchange(bsum, bstat, bpeers, bsend, brecv)
+    pl.when(end)(lambda: pl.semaphore_wait(other_sem, 1))
+
+    @pl.when(border)
+    def _():
+        tell(border_sem, opposite)
+        pl.semaphore_wait(border_sem, len(opposite))
+        tell(run_sem, run)
+
+    for copy in bcopies:
         copy.wait_recv()
-    values, peak, total = combine(zsum, zstat, nz, True)
-
-    l_wo.wait()
+    values, peak, total = combine(bsum, bstat, nz // 2, True)
     mixed[...] = values
     wide = [mixed[pl.ds(h, rows, stride=heads), :] for h in range(heads)]
-    term = dot(jnp.concatenate(wide, axis=1).astype(BF16), wo[...], NT)
+    term = dot(jnp.concatenate(wide, axis=1).astype(BF16), turned[...])
     terms[pl.ds(0, rows), :] = term[:, :lanes]
     terms[pl.ds(rows, rows), :] = jnp.concatenate(
         [term[:, lanes:], jnp.zeros((rows, 2 * lanes - term.shape[1]), F32)], axis=1
     )
-    for k, peer in reversed(list(enumerate(hpeers))):
-        pltpu.make_async_remote_copy(
-            src_ref=terms.at[pl.ds(0, 2 * rows)],
-            dst_ref=terms.at[pl.ds((k + 1) * 2 * rows, 2 * rows)],
-            send_sem=hsend.at[0], recv_sem=hrecv.at[0], device_id=peer, device_id_type=MESH,
-        ).start()
+
+    def send_terms(first, peers):
+        for k, peer in enumerate(peers):
+            pltpu.make_async_remote_copy(
+                src_ref=terms.at[pl.ds(0, 2 * rows)],
+                dst_ref=terms.at[pl.ds((first + k) * 2 * rows, 2 * rows)],
+                send_sem=hsend.at[0], recv_sem=hrecv.at[0], device_id=peer, device_id_type=MESH,
+            ).start()
+
+    pl.when(half == 0)(functools.partial(send_terms, 1 + len(distant), beside))
+    pl.when(jnp.logical_not(border))(lambda: pl.semaphore_wait(run_sem, 1))
+    send_terms(1, distant)
+    pl.when(half == 1)(functools.partial(send_terms, 1 + len(distant), beside))
     others = terms.at[pl.ds(2 * rows, (nhead - 1) * 2 * rows)]
     hcopy = pltpu.make_async_remote_copy(
         src_ref=others, dst_ref=others, send_sem=hsend.at[0], recv_sem=hrecv.at[0],
-        device_id=hpeers[0], device_id_type=MESH,
+        device_id=beside[0], device_id_type=MESH,
     )
     hcopy.wait_recv()
     whole = sum(terms[pl.ds(k * 2 * rows, 2 * rows), :] for k in range(nhead))
     whole = jnp.concatenate([whole[:rows], whole[rows:]], axis=1)
     out_ref[...] = whole[:, : out_ref.shape[1]].astype(out_ref.dtype)
-    for copy in ycopies + zcopies + [hcopy]:
+    for copy in acopies + bcopies + [hcopy]:
         copy.wait_send()
 
 
@@ -233,11 +285,13 @@
     scratch += [
         pltpu.VMEM((w_uv.shape[1] // 128, pairs, 128), F32),
         pltpu.VMEM((pairs, vwidth), F32),
-        pltpu.VMEM((ny * pairs, vwidth), BF16),
-        pltpu.VMEM((ny, 256), F32),
-        pltpu.VMEM((nz * pairs, vwidth), BF16),
-        pltpu.VMEM((nz, 256), F32),
+        pltpu.VMEM(w_o.shape[::-1], BF16),
+        pltpu.VMEM((2 * ny * pairs, vwidth), BF16),
+        pltpu.VMEM((2 * ny, 256), F32),
+        pltpu.VMEM((nz // 2 * pairs, vwidth), BF16),
+        pltpu.VMEM((nz // 2, 256), F32),
         pltpu.VMEM((nhead * 2 * rows, 128), F32),
+        *[pltpu.SemaphoreType.REGULAR] * 4,
         pltpu.SemaphoreType.DMA((len(args) + rows + heads // 2 - 2,)),
     ]
     for n in (2, 2, 1):

time: 38.3 us -> 34.5 us (0.901)
  Pallas kernels: 37.6 us -> 33.8 us
    pallas_call x1, Pallas kernels: 37.6 us -> 33.8 us  [on_device(): pl.pallas_call(functools.partial(kernel, ny, nz, nhead), out_shape=jax.Sh...]
where the time goes in v4:
time: 34.5 us; the launch traced here: 34.4 us
  Pallas kernels  33.8 us (98%)
  local copies, waits for them, and re-layouts  0.58 us (2%)
    pallas_call x1, Pallas kernels, on_device(): pl.pallas_call(functools.partial(kernel, ny, nz, nhead), out_shape=jax.Sh...  33.8 us

profile of v4, /device:TPU:1, one launch (start us, length us, event | category | flops | bytes accessed | tf_op | source)
XLA Modules:
  0.0 34.4 jit_solution(9622120518399143086)
XLA Ops:
  0.0 33.8 %decode.1 = bf16[4,224]{1,0:T(4,128)(2,1)S(1)} custom-call(bf16[4,1024]{1,0:T(4,128)(2,1)} %qn_hbm.1, bf16[4,512]{1,0:T(4,128)(2,1)} %qr_hbm.1, bf16[4,512,512]{2,1,0:T(8,128)(2,1)} %lat_hbm.1, bf16[4,64,512]{2,1,0:T(8,128)(2,1)} %keys_hbm.1, s32[4]{0:T(128)} %len_hbm.1, bf16[8,128,512]{2,1,0:T(8,128)(2,1)} %wuk_hbm.1, bf16[8,512,128]{2,1,0:T(8,128)(2,1)} %wuv_hbm.1, ...), custom_call_target="tpu_custom_call" | custom-call | tf_op jit(solution)/shard_map/decode/pallas_call | solution.py:299
  33.8 0.6 %copy.10 = bf16[4,224]{1,0:T(4,128)(2,1)} copy(bf16[4,224]{1,0:T(4,128)(2,1)S(1)} %decode.1) | data formatting | bytes 3584

commit v5 on v4

--- a/solution.py
+++ b/solution.py
@@ -40,18 +40,17 @@
     loads = [
         pltpu.make_async_copy(src, dst, in_sem.at[n])
         for n, (src, dst) in enumerate(
-            [(qn_hbm, qn)]
-            + [(wuk_hbm.at[pl.ds(2 * h, 2)], wuk.at[pl.ds(2 * h, 2)]) for h in range(heads // 2)]
-            + [(qr_hbm, qr), (len_hbm, lens), (keys_hbm, keys)]
-            + [(lat_hbm.at[r], lat.at[r]) for r in range(rows)]
+            [(qr_hbm, qr), (len_hbm, lens), (keys_hbm, keys), (qn_hbm, qn)]
+            + [(wuk_hbm.at[pl.ds(4 * h, 4)], wuk.at[pl.ds(4 * h, 4)]) for h in range(heads // 4)]
+            + [(lat_hbm.at[pl.ds(r, 2)], lat.at[pl.ds(r, 2)]) for r in range(0, rows, 2)]
             + [(wuv_hbm, wuv), (wo_hbm, wo)]
         )
     ]
     for load in loads:
         load.start()
-    l_qn, l_wuk = loads[0], loads[1 : 1 + heads // 2]
-    l_qr, l_len, l_keys = loads[1 + heads // 2 : 4 + heads // 2]
-    l_lat, l_wuv, l_wo = loads[-2 - rows : -2], loads[-2], loads[-1]
+    l_qr, l_len, l_keys, l_qn = loads[:4]
+    l_wuk = loads[4 : 4 + heads // 4]
+    l_lat, l_wuv, l_wo = loads[-2 - rows // 2 : -2], loads[-2], loads[-1]
 
     y, z = lax.rem(ctx, ny), lax.div(ctx, ny)
     half, core = lax.rem(lax.div(head, 2), 2), lax.rem(head, 2)
@@ -90,26 +89,7 @@
     pl.when(border)(functools.partial(tell, barrier, opposite))
     tell(barrier, apeers + beside)
 
-    l_qn.wait()
-    q = qn[...].astype(F32)
     row_head = iota((heads, 1), 0)
-    q_abs = 0.0
-    for j in range(heads // 2):
-        part = jnp.concatenate(
-            [
-                jnp.concatenate(
-                    [
-                        jnp.where(row_head == h, q[r : r + 1, h * nope : (h + 1) * nope], 0.0)
-                        for h in (2 * j, 2 * j + 1)
-                    ],
-                    axis=1,
-                )
-                for r in range(rows)
-            ],
-            axis=0,
-        ).astype(BF16)
-        l_wuk[j].wait()
-        q_abs += dot(part, wuk[pl.ds(2 * j, 2)].reshape(2 * nope, latent))
     l_qr.wait()
     q = qr[...].astype(F32)
     lane = iota((heads, 2 * rope), 1)
@@ -137,11 +117,33 @@
         mine = slice(r * heads, (r + 1) * heads)
         both = jnp.concatenate([keys[r], keys[r]], axis=0)
         scores.append(dot(rotary[mine].astype(BF16), both))
+    l_qn.wait()
+    q = qn[...].astype(F32)
+    parts = [
+        jnp.concatenate(
+            [
+                jnp.concatenate(
+                    [
+                        jnp.where(row_head == h, q[r : r + 1, h * nope : (h + 1) * nope], 0.0)
+                        for h in (2 * j, 2 * j + 1)
+                    ],
+                    axis=1,
+                )
+                for r in range(rows)
+            ],
+            axis=0,
+        ).astype(BF16)
+        for j in range(heads // 2)
+    ]
+    q_abs = 0.0
+    for j, part in enumerate(parts):
+        if j % 2 == 0:
+            l_wuk[j // 2].wait()
+        q_abs += dot(part, wuk[pl.ds(2 * j, 2)].reshape(2 * nope, latent))
     for r in range(rows):
         mine = slice(r * heads, (r + 1) * heads)
         if r % 2 == 0:
-            l_lat[r].wait()
-            l_lat[r + 1].wait()
+            l_lat[r // 2].wait()
         scores[r] += dot(q_abs[mine].astype(BF16), lat[r], NT)
     scores = jnp.where(valid, jnp.concatenate(scores, axis=0) * scale, LOW)
     peak = jnp.max(scores, axis=1, keepdims=True)
@@ -203,15 +205,16 @@
         if last:
             factor = factor / total
         block = iota((n, lanes), 1) >> (pairs.bit_length() - 1)
-        values = 0.0
+        weights = []
         for g in range(n // per):
             pick = block + g * per == iota((n, lanes), 0)
             row = jnp.sum(jnp.where(pick, factor, 0.0), axis=0, keepdims=True)
-            weights = jnp.where(eye, row, 0.0)
-            high = weights.astype(BF16)
-            low = (weights - high.astype(F32)).astype(BF16)
-            part = sums_ref[pl.ds(g * lanes, lanes), :]
-            values = values + dot(high, part) + dot(low, part)
+            weights.append(jnp.where(eye, row, 0.0))
+        weights = jnp.concatenate(weights, axis=1)
+        high = weights.astype(BF16)
+        low = (weights - high.astype(F32)).astype(BF16)
+        both = dot(jnp.concatenate([high, low], axis=0), sums_ref[...])
+        values = both[:pairs] + both[pairs:]
         return values, peak, total
 
     heard = len(apeers) + len(beside) + middle.astype(jnp.int32) * len(bpeers)
@@ -292,7 +295,7 @@
         pltpu.VMEM((nz // 2, 256), F32),
         pltpu.VMEM((nhead * 2 * rows, 128), F32),
         *[pltpu.SemaphoreType.REGULAR] * 4,
-        pltpu.SemaphoreType.DMA((len(args) + rows + heads // 2 - 2,)),
+        pltpu.SemaphoreType.DMA((len(args) + rows // 2 + heads // 4 - 2,)),
     ]
     for n in (2, 2, 1):
         scratch += [pltpu.SemaphoreType.DMA((n,))] * 2

time: 34.5 us -> 34.4 us (level)
  no operation moved by 1% of the time
where the time goes in v5:
time: 34.4 us; the launch traced here: 34.3 us
  Pallas kernels  33.7 us (98%)
  local copies, waits for them, and re-layouts  0.58 us (2%)
    pallas_call x1, Pallas kernels, on_device(): pl.pallas_call(functools.partial(kernel, ny, nz, nhead), out_shape=jax.Sh...  33.7 us

profile of v5, /device:TPU:1, one launch (start us, length us, event | category | flops | bytes accessed | tf_op | source)
XLA Modules:
  0.0 34.3 jit_solution(11924892588825664398)
XLA Ops:
  0.0 33.7 %decode.1 = bf16[4,224]{1,0:T(4,128)(2,1)S(1)} custom-call(bf16[4,1024]{1,0:T(4,128)(2,1)} %qn_hbm.1, bf16[4,512]{1,0:T(4,128)(2,1)} %qr_hbm.1, bf16[4,512,512]{2,1,0:T(8,128)(2,1)} %lat_hbm.1, bf16[4,64,512]{2,1,0:T(8,128)(2,1)} %keys_hbm.1, s32[4]{0:T(128)} %len_hbm.1, bf16[8,128,512]{2,1,0:T(8,128)(2,1)} %wuk_hbm.1, bf16[8,512,128]{2,1,0:T(8,128)(2,1)} %wuv_hbm.1, ...), custom_call_target="tpu_custom_call" | custom-call | tf_op jit(solution)/shard_map/decode/pallas_call | solution.py:302
  33.7 0.6 %copy.10 = bf16[4,224]{1,0:T(4,128)(2,1)} copy(bf16[4,224]{1,0:T(4,128)(2,1)S(1)} %decode.1) | data formatting | bytes 3584

commit v6 on v5

--- a/solution.py
+++ b/solution.py
@@ -252,28 +252,41 @@
         [term[:, lanes:], jnp.zeros((rows, 2 * lanes - term.shape[1]), F32)], axis=1
     )
 
-    def send_terms(first, peers):
+    def send_terms(first, peers, kind):
         for k, peer in enumerate(peers):
             pltpu.make_async_remote_copy(
                 src_ref=terms.at[pl.ds(0, 2 * rows)],
                 dst_ref=terms.at[pl.ds((first + k) * 2 * rows, 2 * rows)],
-                send_sem=hsend.at[0], recv_sem=hrecv.at[0], device_id=peer, device_id_type=MESH,
+                send_sem=hsend.at[kind], recv_sem=hrecv.at[kind], device_id=peer, device_id_type=MESH,
             ).start()
 
-    pl.when(half == 0)(functools.partial(send_terms, 1 + len(distant), beside))
+    def arrival(first, peers, kind):
+        part = terms.at[pl.ds(first * 2 * rows, len(peers) * 2 * rows)]
+        return pltpu.make_async_remote_copy(
+            src_ref=part, dst_ref=part, send_sem=hsend.at[kind], recv_sem=hrecv.at[kind],
+            device_id=peers[0], device_id_type=MESH,
+        )
+
+    hcopies = [arrival(1, distant, 0), arrival(1 + len(distant), beside, 1)]
+
+    @pl.when(half == 0)
+    def _():
+        send_terms(1 + len(distant), beside, 1)
+        hcopies[1].wait_recv()
+
     pl.when(jnp.logical_not(border))(lambda: pl.semaphore_wait(run_sem, 1))
-    send_terms(1, distant)
-    pl.when(half == 1)(functools.partial(send_terms, 1 + len(distant), beside))
-    others = terms.at[pl.ds(2 * rows, (nhead - 1) * 2 * rows)]
-    hcopy = pltpu.make_async_remote_copy(
-        src_ref=others, dst_ref=others, send_sem=hsend.at[0], recv_sem=hrecv.at[0],
-        device_id=beside[0], device_id_type=MESH,
-    )
-    hcopy.wait_recv()
+    send_terms(1, distant, 0)
+
+    @pl.when(half == 1)
+    def _():
+        send_terms(1 + len(distant), beside, 1)
+        hcopies[1].wait_recv()
+
+    hcopies[0].wait_recv()
     whole = sum(terms[pl.ds(k * 2 * rows, 2 * rows), :] for k in range(nhead))
     whole = jnp.concatenate([whole[:rows], whole[rows:]], axis=1)
     out_ref[...] = whole[:, : out_ref.shape[1]].astype(out_ref.dtype)
-    for copy in acopies + bcopies + [hcopy]:
+    for copy in acopies + bcopies + hcopies:
         copy.wait_send()
 
 
@@ -297,7 +310,7 @@
         *[pltpu.SemaphoreType.REGULAR] * 4,
         pltpu.SemaphoreType.DMA((len(args) + rows // 2 + heads // 4 - 2,)),
     ]
-    for n in (2, 2, 1):
+    for n in (2, 2, 2):
         scratch += [pltpu.SemaphoreType.DMA((n,))] * 2
     return pl.pallas_call(
         functools.partial(kernel, ny, nz, nhead),

time: 34.4 us -> 34.3 us (level)
  no operation moved by 1% of the time
where the time goes in v6:
time: 34.3 us; the launch traced here: 34.2 us
  Pallas kernels  33.6 us (98%)
  local copies, waits for them, and re-layouts  0.58 us (2%)
    pallas_call x1, Pallas kernels, on_device(): pl.pallas_call(functools.partial(kernel, ny, nz, nhead), out_shape=jax.Sh...  33.6 us

profile of v6, /device:TPU:1, one launch (start us, length us, event | category | flops | bytes accessed | tf_op | source)
XLA Modules:
  0.0 34.2 jit_solution(12369413561086196211)
XLA Ops:
  0.0 33.6 %decode.1 = bf16[4,224]{1,0:T(4,128)(2,1)S(1)} custom-call(bf16[4,1024]{1,0:T(4,128)(2,1)} %qn_hbm.1, bf16[4,512]{1,0:T(4,128)(2,1)} %qr_hbm.1, bf16[4,512,512]{2,1,0:T(8,128)(2,1)} %lat_hbm.1, bf16[4,64,512]{2,1,0:T(8,128)(2,1)} %keys_hbm.1, s32[4]{0:T(128)} %len_hbm.1, bf16[8,128,512]{2,1,0:T(8,128)(2,1)} %wuk_hbm.1, bf16[8,512,128]{2,1,0:T(8,128)(2,1)} %wuv_hbm.1, ...), custom_call_target="tpu_custom_call" | custom-call | tf_op jit(solution)/shard_map/decode/pallas_call | solution.py:315
  33.6 0.6 %copy.10 = bf16[4,224]{1,0:T(4,128)(2,1)} copy(bf16[4,224]{1,0:T(4,128)(2,1)S(1)} %decode.1) | data formatting | bytes 3584

commit v7 on v5

--- a/solution.py
+++ b/solution.py
@@ -262,7 +262,15 @@
 
     pl.when(half == 0)(functools.partial(send_terms, 1 + len(distant), beside))
     pl.when(jnp.logical_not(border))(lambda: pl.semaphore_wait(run_sem, 1))
-    send_terms(1, distant)
+    for x in range(nhead // 4):
+        for c in (1, 0):
+            k, j = lax.rem(x - column + nhead // 4, nhead // 4), lax.rem(c - core + 2, 2)
+            pltpu.make_async_remote_copy(
+                src_ref=terms.at[pl.ds(0, 2 * rows)],
+                dst_ref=terms.at[pl.ds(pl.multiple_of((1 + 2 * k + j) * 2 * rows, 2 * rows), 2 * rows)],
+                send_sem=hsend.at[0], recv_sem=hrecv.at[0],
+                device_id={"ctx": ctx, "head": x * 4 + (1 - half) * 2 + c}, device_id_type=MESH,
+            ).start()
     pl.when(half == 1)(functools.partial(send_terms, 1 + len(distant), beside))
     others = terms.at[pl.ds(2 * rows, (nhead - 1) * 2 * rows)]
     hcopy = pltpu.make_async_remote_copy(

time: 34.4 us -> 34.3 us (level)
  no operation moved by 1% of the time
where the time goes in v7:
time: 34.3 us; the launch traced here: 34.2 us
  Pallas kernels  33.6 us (98%)
  local copies, waits for them, and re-layouts  0.58 us (2%)
    pallas_call x1, Pallas kernels, on_device(): pl.pallas_call(functools.partial(kernel, ny, nz, nhead), out_shape=jax.Sh...  33.6 us

profile of v7, /device:TPU:1, one launch (start us, length us, event | category | flops | bytes accessed | tf_op | source)
XLA Modules:
  0.0 34.2 jit_solution(13262956199406638185)
XLA Ops:
  0.0 33.6 %decode.1 = bf16[4,224]{1,0:T(4,128)(2,1)S(1)} custom-call(bf16[4,1024]{1,0:T(4,128)(2,1)} %qn_hbm.1, bf16[4,512]{1,0:T(4,128)(2,1)} %qr_hbm.1, bf16[4,512,512]{2,1,0:T(8,128)(2,1)} %lat_hbm.1, bf16[4,64,512]{2,1,0:T(8,128)(2,1)} %keys_hbm.1, s32[4]{0:T(128)} %len_hbm.1, bf16[8,128,512]{2,1,0:T(8,128)(2,1)} %wuk_hbm.1, bf16[8,512,128]{2,1,0:T(8,128)(2,1)} %wuv_hbm.1, ...), custom_call_target="tpu_custom_call" | custom-call | tf_op jit(solution)/shard_map/decode/pallas_call | solution.py:310
  33.6 0.6 %copy.10 = bf16[4,224]{1,0:T(4,128)(2,1)} copy(bf16[4,224]{1,0:T(4,128)(2,1)S(1)} %decode.1) | data formatting | bytes 3584
